TPU v7x, 32 devices: a whole 2x2x4 slice. The times are simulated.
32 devices in a mesh: groups: 2 (over x), section: 16 (over z, y, core).
Axes of the slice: x: 2, y: 2, z: 4, core: 2. Of those that a mesh axis runs over, the one named last changes fastest.
Arguments:
- feats: bfloat16 [256, 24576], P('groups', 'section'), parts along dimension 0, may hold values from -6 to 6
- uniting_weight: bfloat16 [24576, 8192], P('section'), may hold values from -0.0546875 to 0.0546875
- embeds_verified: bfloat16 [256, 8192], P('groups', 'section'), parts along dimension 0, may hold values from -6 to 6
- draft_embeds: bfloat16 [4, 256, 8192], P(None, 'groups', 'section'), parts along dimension 1, may hold values from -6 to 6
- gain_embed: bfloat16 [8192], P('section'), may hold values from 0.25 to 1.75
- gain_hidden: bfloat16 [8192], P('section'), may hold values from 0.25 to 1.75
- proj_embed: bfloat16 [8192, 5120], P('section'), may hold values from -0.0625 to 0.0625
- proj_hidden: bfloat16 [8192, 5120], P('section'), may hold values from -0.0625 to 0.0625
- out_proj: bfloat16 [4096, 8192], P(None, 'section'), may hold values from -0.09375 to 0.09375
- lengths: int32 [32], P('groups'), parts along dimension 0, may hold values from 1 to 32, 128 in all
- root_seq: int32 [256], P('groups'), parts along dimension 0, may hold values from 0 to 15
- parents: int32 [3, 256], P(None, 'groups'), parts along dimension 1, may hold values from 0 to 127
Outputs:
- drafts: bfloat16 [1024, 8192], P(('groups', 'section')), parts along dimension 0
There are 2 independent parts, one for each index of `groups`. A program takes and returns all parts, laid end to end along the dimension named above; an argument that names none is the same for every part. Nothing has to cross between parts.
Inputs may be any that keep to these rules, and one draw needn't show every extreme that they name: `lengths`: sum to 128; the largest is exactly 32.
All inputs are finite; a program needn't handle non-finite values.
Results may differ from a plain program's by a relative error of at most 0.012.
Values may be sent and summed in bfloat16 or wider, within the bound.
A program may use at most 128 MiB of HBM per device.

v0:
```python
import math

import jax
import jax.numpy as jnp
from jax import lax
from jax.sharding import PartitionSpec as P

D = 8192
HD = 128


def rope_heads(values, positions):
    half = values.shape[-1] // 2
    freq = 500000.0 ** (-(jnp.arange(half, dtype=jnp.float32) * 2.0 / values.shape[-1]))
    angle = positions.astype(jnp.float32)[:, None] * freq[None, :]
    cosine = jnp.cos(angle)[:, None, :]
    sine = jnp.sin(angle)[:, None, :]
    first = values[..., :half]
    second = values[..., half:]
    return jnp.concatenate(
        [first * cosine - second * sine, second * cosine + first * sine], axis=-1
    )


def scaled_input(values, gain):
    return (values.astype(jnp.float32) * gain.astype(jnp.float32)[None, :]).astype(jnp.bfloat16)


def project_rows(embed_rows, hidden_rows, gain_embed, gain_hidden, w_embed, w_hidden):
    part_e = jnp.dot(
        scaled_input(embed_rows, gain_embed), w_embed, preferred_element_type=jnp.float32
    )
    part_h = jnp.dot(
        scaled_input(hidden_rows, gain_hidden), w_hidden, preferred_element_type=jnp.float32
    )
    square_e = jnp.sum(embed_rows.astype(jnp.float32) ** 2, axis=-1)
    square_h = jnp.sum(hidden_rows.astype(jnp.float32) ** 2, axis=-1)
    total_e, total_h = lax.psum((square_e, square_h), "section")
    inv_e = lax.rsqrt(total_e / D + 1e-05)
    inv_h = lax.rsqrt(total_h / D + 1e-05)
    return lax.psum(part_e * inv_e[:, None] + part_h * inv_h[:, None], "section")


def attend(queries, keys, values, allowed):
    nodes = queries.shape[0]
    kv_heads = keys.shape[1]
    group = queries.shape[1] // kv_heads
    grouped = queries.reshape(nodes, kv_heads, group, queries.shape[2])
    scores = jnp.einsum(
        "bkgd,nkd->bkgn", grouped, keys, preferred_element_type=jnp.float32
    ) / math.sqrt(queries.shape[2])
    scores = jnp.where(allowed[:, None, None, :], scores, -1e30)
    top = jnp.max(scores, axis=-1, keepdims=True)
    expo = jnp.exp(scores - top)
    weights = (expo / jnp.sum(expo, axis=-1, keepdims=True)).astype(jnp.bfloat16)
    mixed = jnp.einsum("bkgn,nkd->bkgd", weights, values, preferred_element_type=jnp.float32)
    return mixed.astype(jnp.bfloat16).reshape(nodes, -1)


def local(
    feats,
    uniting_weight,
    embeds_verified,
    draft_embeds,
    gain_embed,
    gain_hidden,
    proj_embed,
    proj_hidden,
    out_proj,
    lengths,
    root_seq,
    parents,
):
    row_count = feats.shape[0]
    node_count = draft_embeds.shape[1]
    step_count = draft_embeds.shape[0]
    qcols = out_proj.shape[0]
    kcols = (proj_embed.shape[1] - qcols) // 2
    q_heads = qcols // HD
    kv_heads = kcols // HD
    ends = jnp.cumsum(lengths)
    starts = ends - lengths
    row_ids = jnp.arange(row_count, dtype=jnp.int32)
    seg = jnp.sum((row_ids[:, None] >= ends[None, :]).astype(jnp.int32), axis=1)
    pos_v = row_ids - starts[seg]
    last = ends - 1
    partial_value = jnp.dot(feats, uniting_weight, preferred_element_type=jnp.float32)
    united = lax.psum_scatter(partial_value, "section", scatter_dimension=1, tiled=True).astype(
        jnp.bfloat16
    )
    context = project_rows(
        embeds_verified,
        united,
        gain_embed,
        gain_hidden,
        proj_embed[:, qcols:],
        proj_hidden[:, qcols:],
    )
    keys_v = rope_heads(context[:, :kcols].reshape(row_count, kv_heads, HD), pos_v).astype(
        jnp.bfloat16
    )
    vals_v = context[:, kcols:].reshape(row_count, kv_heads, HD).astype(jnp.bfloat16)
    node_ids = jnp.arange(node_count, dtype=jnp.int32)
    node_keys = []
    node_vals = []
    ancestors = []
    drafts = []
    seq = root_seq
    h_out = united
    for step in range(step_count):
        if step == 0:
            h_in = jnp.take(united, last[root_seq], axis=0)
        else:
            link = parents[step - 1]
            h_in = jnp.take(h_out, link, axis=0)
            seq = seq[link]
            ancestors = [older[link] for older in ancestors] + [link]
        positions = lengths[seq] + step
        proj = project_rows(
            draft_embeds[step], h_in, gain_embed, gain_hidden, proj_embed, proj_hidden
        )
        queries = rope_heads(proj[:, :qcols].reshape(node_count, q_heads, HD), positions).astype(
            jnp.bfloat16
        )
        node_keys.append(
            rope_heads(
                proj[:, qcols : qcols + kcols].reshape(node_count, kv_heads, HD), positions
            ).astype(jnp.bfloat16)
        )
        node_vals.append(
            proj[:, qcols + kcols :].reshape(node_count, kv_heads, HD).astype(jnp.bfloat16)
        )
        masks = [seg[None, :] == seq[:, None]]
        for older in ancestors:
            masks.append(older[:, None] == node_ids[None, :])
        masks.append(node_ids[:, None] == node_ids[None, :])
        allowed = jnp.concatenate(masks, axis=1)
        keys = jnp.concatenate([keys_v] + node_keys, axis=0)
        values = jnp.concatenate([vals_v] + node_vals, axis=0)
        mixed = attend(queries, keys, values, allowed)
        h_out = (
            h_in.astype(jnp.float32) + jnp.dot(mixed, out_proj, preferred_element_type=jnp.float32)
        ).astype(jnp.bfloat16)
        drafts.append(h_out)
    columns = jnp.concatenate(drafts, axis=0)
    return lax.all_to_all(columns, "section", split_axis=0, concat_axis=1, tiled=True)


def solution(mesh):
    return jax.shard_map(
        local,
        mesh=mesh,
        in_specs=(
            P("groups", "section"),
            P("section", None),
            P("groups", "section"),
            P(None, "groups", "section"),
            P("section"),
            P("section"),
            P("section", None),
            P("section", None),
            P(None, "section"),
            P("groups"),
            P("groups"),
            P(None, "groups"),
        ),
        out_specs=P(("groups", "section"), None),
        check_vma=False,
    )
```

profile of v0, /device:TPU:31, one launch (start us, length us, event | category | flops | bytes accessed | tf_op | source)
XLA Modules:
  0.0 757.9 jit_solution(1698928968770939692)
XLA Ops:
  7.5 13.6 %fusion.205 = f32[128,8192]{1,0:T(8,128)} fusion(bf16[128,1536]{1,0:T(8,128)(2,1)S(1)} %copy-done, bf16[1536,8192]{1,0:T(8,128)(2,1)} %param.15), kind=kOutput, calls=%fused_computation.444 | convolution fusion | flops 3221225472 | bytes 29753344 | tf_op jit(solution)/shard_map/dot_general | solution.py:87
  27.7 10.1 %compare_and_fusion.3 = (pred[128]{0:T(512)(128)(4,1)S(1)}, s32[128]{0:T(128)S(1)}) fusion(s32[]{:T(128)} %bitcast.16, s32[]{:T(128)} %bitcast.15, s32[]{:T(128)} %bitcast.14, s32[]{:T(128)} %bitcast.13, s32[]{:T(128)} %bitcast.12, s32[]{:T(128)} %bitcast.11, s32[]{:T(128)} %bitcast.10, s32[]{:T(128)} %bitcast.9, s32[]{:T(128)} %bitcast.8, s32[]{:T(128)} %bitcast.7, ...), kind=kLoop, calls=%fused_computation.329 | loop fusion | flops 4992 | bytes 1216 | tf_op jit(solution)/shard_map/jit(_take)/and | solution.py:112
  41.0 50.6 %reduce-scatter.2.cloned.1.call-done = f32[128,512]{1,0:T(8,128)} async-done(((f32[128,8192]{1,0:T(8,128)}), f32[128,512]{1,0:T(8,128)}) %reduce-scatter.2.cloned.1.call-update) | async-done | bytes 262160 | tf_op jit(solution)/shard_map/reduce_scatter | solution.py:88
  93.7 29.0 %all-reduce.3 = (f32[128]{0:T(128)S(1)}, f32[128]{0:T(128)S(1)}, f32[128]{0:T(128)S(1)}, f32[128]{0:T(128)S(1)}) all-reduce(f32[128]{0:T(128)S(1)} %get-tuple-element.30, f32[128]{0:T(128)S(1)} %fusion.96, f32[128]{0:T(128)S(1)} %fusion.108, f32[128]{0:T(128)S(1)} %get-tuple-element.7), channel_id=1, replica_groups=mesh['groups'=2,'section'=16] {'section'}, use_global_device_ids=true, to_apply=%region_5.7 | all-reduce | flops 512 | bytes 4096 | tf_op jit(solution)/shard_map/psum | solution.py:38
  124.3 3.5 convolution_multiply_fusion.6
  129.0 2.4 fusion.6
  132.6 10.2 %fusion.163 = f32[128]{0:T(128)S(1)} fusion(s32[128]{0:T(128)S(1)} %gather_fusion.1, s32[]{:T(128)} %bitcast.57, s32[]{:T(128)} %bitcast.58, s32[]{:T(128)} %bitcast.59, s32[]{:T(128)} %bitcast.60, s32[]{:T(128)} %bitcast.61, s32[]{:T(128)} %bitcast.63, s32[]{:T(128)} %bitcast.62, s32[]{:T(128)} %bitcast.48, s32[]{:T(128)} %bitcast.49, s32[]{:T(128)} %bitcast.50, ...), kind=kLoop, calls=%fused_computation.393 | loop fusion | flops 4480 | bytes 1088 | tf_op jit(solution)/shard_map/convert_element_type | solution.py:15
  142.7 10.1 %fusion.165 = f32[128]{0:T(128)S(1)} fusion(s32[128]{0:T(128)S(1)} %gather_fusion.3, s32[]{:T(128)} %bitcast.57, s32[]{:T(128)} %bitcast.58, s32[]{:T(128)} %bitcast.59, s32[]{:T(128)} %bitcast.60, s32[]{:T(128)} %bitcast.61, s32[]{:T(128)} %bitcast.63, s32[]{:T(128)} %bitcast.62, s32[]{:T(128)} %bitcast.48, s32[]{:T(128)} %bitcast.49, s32[]{:T(128)} %bitcast.50, ...), kind=kLoop, calls=%fused_computation.395 | loop fusion | flops 4480 | bytes 1088 | tf_op jit(solution)/shard_map/convert_element_type | solution.py:15
  152.9 10.2 %fusion.161 = f32[128]{0:T(128)S(1)} fusion(s32[128]{0:T(128)S(1)} %gather_fusion, s32[]{:T(128)} %bitcast.57, s32[]{:T(128)} %bitcast.58, s32[]{:T(128)} %bitcast.59, s32[]{:T(128)} %bitcast.60, s32[]{:T(128)} %bitcast.61, s32[]{:T(128)} %bitcast.63, s32[]{:T(128)} %bitcast.62, s32[]{:T(128)} %bitcast.48, s32[]{:T(128)} %bitcast.49, s32[]{:T(128)} %bitcast.50, ...), kind=kLoop, calls=%fused_computation.391 | loop fusion | flops 4480 | bytes 1088 | tf_op jit(solution)/shard_map/convert_element_type | solution.py:15
  163.1 10.1 %fusion.154 = f32[128]{0:T(128)S(1)} fusion(s32[]{:T(128)} %bitcast.48, s32[]{:T(128)} %bitcast.49, s32[]{:T(128)} %bitcast.50, s32[]{:T(128)} %bitcast.51, s32[]{:T(128)} %bitcast.52, s32[]{:T(128)} %bitcast.53, s32[]{:T(128)} %bitcast.54, s32[]{:T(128)} %bitcast.55, s32[]{:T(128)} %bitcast.56, s32[]{:T(128)} %bitcast.57, s32[]{:T(128)} %bitcast.58, ...), kind=kLoop, calls=%fused_computation.384 | loop fusion | flops 4352 | bytes 1088 | tf_op jit(solution)/shard_map/convert_element_type | solution.py:15
  173.2 9.9 %fusion.169 = f32[128]{0:T(128)S(1)} fusion(s32[128]{0:T(128)S(1)} %convert_reduce_fusion, s32[]{:T(128)} %bitcast.40, s32[]{:T(128)} %bitcast.41, s32[]{:T(128)} %bitcast.42, s32[]{:T(128)} %bitcast.43, s32[]{:T(128)} %bitcast.44, s32[]{:T(128)} %bitcast.46, s32[]{:T(128)} %bitcast.45, s32[]{:T(128)} %bitcast.23, s32[]{:T(128)} %bitcast.25, s32[]{:T(128)} %bitcast.27, ...), kind=kLoop, calls=%fused_computation.406 | loop fusion | flops 4480 | bytes 1088 | tf_op jit(solution)/shard_map/convert_element_type | solution.py:15
  183.1 2.0 multiply_cosine_fusion
  185.1 48.0 %all-reduce.16.cloned.1.call-done = (f32[128,1024]{1,0:T(8,128)}, f32[128,5120]{1,0:T(8,128)}) async-done(((f32[128,1024]{1,0:T(8,128)}, f32[128,5120]{1,0:T(8,128)}), (f32[128,1024]{1,0:T(8,128)}, f32[128,5120]{1,0:T(8,128)})) %all-reduce.16.cloned.1.call-update) | async-done | bytes 3145744 | tf_op jit(solution)/shard_map/psum | solution.py:41
  237.0 3.2 slice_bitcast_fusion.3
  241.8 2.0 copy.155
  253.3 29.0 %all-reduce.2 = (f32[128]{0:T(128)S(1)}, f32[128]{0:T(128)S(1)}) all-reduce(f32[128]{0:T(128)S(1)} %fusion.110, f32[128]{0:T(128)S(1)} %copy-done.63), channel_id=1, replica_groups=mesh['groups'=2,'section'=16] {'section'}, use_global_device_ids=true, to_apply=%region_18.20 | all-reduce | flops 256 | bytes 2048 | tf_op jit(solution)/shard_map/psum | solution.py:38
  282.3 3.5 convolution_multiply_fusion.4
  286.3 2.4 fusion.7
  291.4 96.5 %all-reduce.10.cloned.1.call-done = f32[128,5120]{1,0:T(8,128)} async-done(((f32[128,5120]{1,0:T(8,128)}), f32[128,5120]{1,0:T(8,128)}) %all-reduce.10.cloned.1.call-update) | async-done | bytes 2621456 | tf_op jit(solution)/shard_map/psum | solution.py:41
  410.3 29.0 %all-reduce.1 = (f32[128]{0:T(128)S(1)}, f32[128]{0:T(128)S(1)}) all-reduce(f32[128]{0:T(128)S(1)} %fusion.112, f32[128]{0:T(128)S(1)} %copy-done.62), channel_id=1, replica_groups=mesh['groups'=2,'section'=16] {'section'}, use_global_device_ids=true, to_apply=%region_25.27 | all-reduce | flops 256 | bytes 2048 | tf_op jit(solution)/shard_map/psum | solution.py:38
  439.3 3.5 convolution_multiply_fusion.2
  443.3 2.4 fusion.8
  451.4 93.5 %all-reduce.12.cloned.1.call-done = f32[128,5120]{1,0:T(8,128)} async-done(((f32[128,5120]{1,0:T(8,128)}), f32[128,5120]{1,0:T(8,128)}) %all-reduce.12.cloned.1.call-update) | async-done | bytes 2621456 | tf_op jit(solution)/shard_map/psum | solution.py:41
  554.0 2.7 subtract_convert_fusion.1
  563.2 3.5 fusion.199
  570.8 29.2 %all-reduce = (f32[128]{0:T(128)S(1)}, f32[128]{0:T(128)S(1)}) all-reduce(f32[128]{0:T(128)S(1)} %fusion.114, f32[128]{0:T(128)S(1)} %copy-done.61), channel_id=1, replica_groups=mesh['groups'=2,'section'=16] {'section'}, use_global_device_ids=true, to_apply=%region_32.34 | all-reduce | flops 256 | bytes 2048 | tf_op jit(solution)/shard_map/psum | solution.py:38
  600.0 3.5 convolution_multiply_fusion
  604.0 2.4 fusion.9
  609.9 95.8 %all-reduce.14.cloned.1.call-done = f32[128,5120]{1,0:T(8,128)} async-done(((f32[128,5120]{1,0:T(8,128)}), f32[128,5120]{1,0:T(8,128)}) %all-reduce.14.cloned.1.call-update) | async-done | bytes 2621456 | tf_op jit(solution)/shard_map/psum | solution.py:41
  714.9 8.8 %fusion.200 = (f32[128,4,8]{0,2,1:T(8,128)S(1)}, f32[128,4,8,640]{0,3,2,1:T(8,128)}) fusion(pred[128,640]{0,1:T(8,128)(4,1)} %constant_dynamic-update-slice_fusion.5, bf16[640,4,128]{2,0,1:T(8,128)(2,1)} %maximum_dynamic-update-slice_fusion, bf16[128,4,8,64]{3,0,2,1:T(8,128)(2,1)S(1)} %bitcast.603, bf16[128,4,8,64]{3,0,2,1:T(8,128)(2,1)S(1)} %bitcast.602), kind=kOutput, calls=%fused_computation.443 | convolution fusion | flops 683672192 | bytes 12288000 | tf_op jit(solution)/shard_map/sub | solution.py:54
  723.7 5.3 fusion.31
  729.9 20.2 %all_to_all.19 = bf16[16,32,512]{2,1,0:T(8,128)(2,1)S(1)} all-to-all(bf16[16,32,512]{2,1,0:T(8,128)(2,1)S(1)} %bitcast.600), channel_id=1, replica_groups=mesh['groups'=2,'section'=16] {'section'}, dimensions={0} | all-to-all | bytes 1048576 | tf_op jit(solution)/shard_map/all_to_all | solution.py:146
  (293 shorter events, 96.7 us)
Async XLA Ops:
  6.5 85.0 %reduce-scatter.2.cloned.1.call-start = ((), (), s32[]{:S(2)}) async-start(), calls=%async_computation.2 | async-start | bytes 4456448 | tf_op jit(solution)/shard_map/reduce_scatter | solution.py:88
  21.1 18.3 %copy-start.26 = (bf16[128,512]{1,0:T(8,128)(2,1)S(1)}, bf16[128,512]{1,0:T(8,128)(2,1)}, u32[]{:S(2)}) copy-start(bf16[128,512]{1,0:T(8,128)(2,1)} %param.16) | copy-start | bytes 393220
  21.1 18.4 %copy-start.7 = (bf16[4,128,512]{2,1,0:T(8,128)(2,1)S(1)}, bf16[4,128,512]{2,1,0:T(8,128)(2,1)}, u32[]{:S(2)}) copy-start(bf16[4,128,512]{2,1,0:T(8,128)(2,1)} %param.17) | copy-start | bytes 1572868
  21.2 212.0 %all-reduce.16.cloned.1.call-start = ((), (), s32[]{:S(2)}) async-start(), calls=%async_computation.6 | async-start | bytes 6291456 | tf_op jit(solution)/shard_map/psum | solution.py:41
  37.8 90.0 %copy-start.50 = (pred[128]{0:T(512)(128)(4,1)}, pred[128]{0:T(512)(128)(4,1)S(1)}, u32[]{:S(2)}) copy-start(pred[128]{0:T(512)(128)(4,1)S(1)} %get-tuple-element.28) | copy-start | bytes 388
  37.8 94.1 %copy-start.38 = (pred[128,128]{0,1:T(8,128)(4,1)}, pred[128,128]{0,1:T(8,128)(4,1)S(1)}, u32[]{:S(2)}) copy-start(pred[128,128]{0,1:T(8,128)(4,1)S(1)} %iota_compare_fusion.6) | copy-start | bytes 49156
  122.6 5.2 slice-start
  131.4 256.5 %all-reduce.10.cloned.1.call-start = ((), (), s32[]{:S(2)}) async-start(), calls=%async_computation.3 | async-start | bytes 5242880 | tf_op jit(solution)/shard_map/psum | solution.py:41
  253.1 32.7 %copy-start.12 = (bf16[128,512]{1,0:T(8,128)(2,1)}, bf16[128,512]{1,0:T(8,128)(2,1)S(1)}, u32[]{:S(2)}) copy-start(bf16[128,512]{1,0:T(8,128)(2,1)S(1)} %gather_fusion.7) | copy-start | bytes 393220
  282.2 3.7 slice-start.2
  282.3 4.0 slice-start.3
  286.3 4.5 copy-start.39
  286.3 4.5 copy-start.42
  288.8 256.2 %all-reduce.12.cloned.1.call-start = ((), (), s32[]{:S(2)}) async-start(), calls=%async_computation.4 | async-start | bytes 5242880 | tf_op jit(solution)/shard_map/psum | solution.py:41
  389.7 7.3 copy-start.21
  389.7 7.3 copy-start.22
  398.9 4.1 copy-start.23
  410.1 32.8 %copy-start.10 = (bf16[128,512]{1,0:T(8,128)(2,1)}, bf16[128,512]{1,0:T(8,128)(2,1)S(1)}, u32[]{:S(2)}) copy-start(bf16[128,512]{1,0:T(8,128)(2,1)S(1)} %gather_fusion.8) | copy-start | bytes 393220
  439.3 4.0 slice-start.5
  445.8 4.4 copy-start.56
  445.8 4.4 copy-start.43
  445.8 4.4 copy-start.44
  445.8 259.9 %all-reduce.14.cloned.1.call-start = ((), (), s32[]{:S(2)}) async-start(), calls=%async_computation.5 | async-start | bytes 5242880 | tf_op jit(solution)/shard_map/psum | solution.py:41
  546.7 7.3 copy-start.20
  556.7 5.1 copy-start.15
  556.7 5.1 copy-start.17
  570.6 33.0 %copy-start.8 = (bf16[128,512]{1,0:T(8,128)(2,1)}, bf16[128,512]{1,0:T(8,128)(2,1)S(1)}, u32[]{:S(2)}) copy-start(bf16[128,512]{1,0:T(8,128)(2,1)S(1)} %gather_fusion.9) | copy-start | bytes 393220
  600.0 4.0 slice-start.7
  609.9 96.9 %copy-start.47 = (bf16[640,4,128]{2,0,1:T(8,128)(2,1)}, bf16[640,4,128]{2,0,1:T(8,128)(2,1)S(1)}, u32[]{:S(2)}) copy-start(bf16[640,4,128]{2,0,1:T(8,128)(2,1)S(1)} %maximum_dynamic-update-slice_fusion.1) | copy-start | bytes 1966084
  723.7 5.4 copy-start.6
  723.7 5.4 copy-start.9
  729.0 21.9 %copy-start.1 = (bf16[128,1536]{1,0:T(8,128)(2,1)S(1)}, bf16[128,1536]{1,0:T(8,128)(2,1)}, u32[]{:S(2)}) copy-start(bf16[128,1536]{1,0:T(8,128)(2,1)} %param.14) | copy-start | bytes 1179652
  (46 other events, 96.5 us)
Sparse Core Ops, SparseCore 0:
  21.3 70.2 reduce-scatter.1
  131.6 101.5 all-reduce.15
  288.9 99.0 all-reduce.9
  445.9 99.0 all-reduce.11
  606.6 99.0 all-reduce.13
where the time goes:
time: 769 us; the launch traced here: 758 us
  waiting for transfers between devices  385 us (50%)
  blocking collectives  136 us (18%)
  other arithmetic  90.1 us (12%)
  local copies, waits for them, and re-layouts  68.1 us (9%)
  matrix products  62.8 us (8%)
  between operations  15 us (2%)
    psum x4, waiting for transfers between devices, project_rows(): lax.psum(part_e * inv_e[:, None] + part_h * inv_h[:, None], 'section')  334 us
    psum x4, blocking collectives, project_rows(): total_e, total_h = lax.psum((square_e, square_h), 'section')  116 us
    reduce_scatter x1, waiting for transfers between devices, local(): lax.psum_scatter(partial_value, 'section', scatter_dimension=1, tiled=True)  50.6 us
    convert_element_type x5, other arithmetic, rope_heads(): angle = positions.astype(jnp.float32)[:, None] * freq[None, :]  50.5 us
    unnamed x162, local copies, waits for them, and re-layouts  24.5 us
    all_to_all x1, blocking collectives, local(): lax.all_to_all(columns, 'section', split_axis=0, concat_axis=1, tiled=True)  20.2 us
    dot_general x5, matrix products, project_rows(): jnp.dot(scaled_input(hidden_rows, gain_hidden), w_hidden, preferred_eleme...  15.8 us
  transfers between devices with their start and end apart: 5, of which 5 were waited for; matrix products, arithmetic and copies ran while one was open for 11% of the time, Pallas kernels for 0%

commit v1 on v0

--- a/solution.py
+++ b/solution.py
@@ -1,8 +1,11 @@
+import functools
 import math
 
 import jax
 import jax.numpy as jnp
 from jax import lax
+from jax.experimental import pallas as pl
+from jax.experimental.pallas import tpu as pltpu
 from jax.sharding import PartitionSpec as P
 
 D = 8192
@@ -57,7 +60,7 @@
     return mixed.astype(jnp.bfloat16).reshape(nodes, -1)
 
 
-def local(
+def local_plain(
     feats,
     uniting_weight,
     embeds_verified,
@@ -146,9 +149,540 @@
     return lax.all_to_all(columns, "section", split_axis=0, concat_axis=1, tiled=True)
 
 
+Z, Y, C = 4, 2, 2
+N = Z * Y * C
+MASKED = -1e30
+
+
+def remote(src, dst, send, recv, peer):
+    return pltpu.make_async_remote_copy(
+        src_ref=src,
+        dst_ref=dst,
+        send_sem=send,
+        recv_sem=recv,
+        device_id={"section": peer},
+        device_id_type=pl.DeviceIdType.MESH,
+    )
+
+
+def column_to_row(column):
+    rows = lax.broadcasted_iota(jnp.int32, (column.shape[0], column.shape[0]), 0)
+    cols = lax.broadcasted_iota(jnp.int32, (column.shape[0], column.shape[0]), 1)
+    return jnp.sum(jnp.where(rows == cols, column, 0.0), axis=0, keepdims=True)
+
+
+def row_to_column(pick, row):
+    return jnp.sum(jnp.where(pick > 0, row, 0.0), axis=1, keepdims=True)
+
+
+def draft_kernel(
+    steps,
+    partial_ref,
+    eg_ref,
+    sqe_ref,
+    gh_ref,
+    we_ref,
+    wh_ref,
+    wo_ref,
+    pick_ref,
+    mask_ref,
+    cos_ref,
+    sin_ref,
+    out_ref,
+    h_ref,
+    hg_ref,
+    part_ref,
+    kvp_ref,
+    own_ref,
+    cs_ref,
+    cr_ref,
+    ys_ref,
+    yr_ref,
+    zs_ref,
+    zr_ref,
+    uown_ref,
+    ucs_ref,
+    ucr_ref,
+    uys_ref,
+    uyr_ref,
+    uzs_ref,
+    uzr_ref,
+    sqs_ref,
+    sqr_ref,
+    kv_ref,
+    att_ref,
+    sum_ref,
+    inve_ref,
+    cs_sem,
+    cr_sem,
+    ys_sem,
+    yr_sem,
+    zs_sem,
+    zr_sem,
+    sqs_sem,
+    sqr_sem,
+    kvs_sem,
+    kvr_sem,
+    ags_sem,
+    agr_sem,
+):
+    rows, width = h_ref.shape
+    me = lax.axis_index("section")
+    z = me // 4
+    y = (me // 2) % 2
+    c = me % 2
+    yc = me % 4
+    sibling = z * 4 + y * 2 + (1 - c)
+    y_peer = z * 4 + (1 - y) * 2 + c
+    quarter = rows // 4
+    qcols = wo_ref.shape[0]
+    kcols = (we_ref.shape[1] - qcols) // 2
+    block_cols = qcols // N
+    f32, bf16 = jnp.float32, jnp.bfloat16
+
+    kv_ref[...] = jnp.zeros_like(kv_ref)
+
+    barrier = pltpu.get_barrier_semaphore()
+
+    def greet(k, _):
+        pl.semaphore_signal(
+            barrier,
+            inc=1,
+            device_id={"section": (me + k) % N},
+            device_id_type=pl.DeviceIdType.MESH,
+        )
+        return 0
+
+    lax.fori_loop(1, N, greet, 0)
+    pl.semaphore_wait(barrier, N - 1)
+
+    def squares_copy(slot, k, peer, source):
+        return remote(
+            sqs_ref.at[slot],
+            sqr_ref.at[slot, source],
+            sqs_sem.at[slot, k],
+            sqr_sem.at[slot, source],
+            peer,
+        )
+
+    def squares_start(slot, value):
+        sqs_ref[slot] = value
+        sqr_ref[slot, me] = value
+
+        def go(k, _):
+            squares_copy(slot, k, (me + k) % N, me).start()
+            return 0
+
+        lax.fori_loop(1, N, go, 0)
+
+    def squares_total(slot):
+        def go(k, total):
+            source = (me + k) % N
+            copy = squares_copy(slot, k, source, source)
+            copy.wait_recv()
+            copy.wait_send()
+            return total + sqr_ref[slot, source]
+
+        return lax.fori_loop(1, N, go, sqr_ref[slot, me])
+
+    def reduce_scatter(s, t, size, block, own, cs, cr, ys, yr, zs, zr):
+        def order(k):
+            far = k < 4
+            return jnp.where(far, k, k - 4), jnp.where(far, 1 - y, y)
+
+        def core_copy(k):
+            return remote(
+                cs.at[k, pl.ds(0, size)], cr.at[t, k, pl.ds(0, size)], cs_sem.at[s, k],
+                cr_sem.at[s, k], sibling,
+            )
+
+        def y_copy(k):
+            return remote(
+                ys.at[k, pl.ds(0, size)], yr.at[t, k, pl.ds(0, size)], ys_sem.at[s, k],
+                yr_sem.at[s, k], y_peer,
+            )
+
+        def z_copy(k):
+            other = (z + k) % Z
+            return remote(
+                zs.at[k, pl.ds(0, size)], zr.at[t, k, pl.ds(0, size)], zs_sem.at[s, k],
+                zr_sem.at[s, k], other * 4 + yc,
+            )
+
+        def give(k, _):
+            zb, yb = order(k)
+            block(zb, yb, 1 - c, cs.at[k], bf16)
+            core_copy(k).start()
+            return 0
+
+        lax.fori_loop(0, 8, give, 0)
+
+        def keep(k, _):
+            zb, yb = order(k)
+            block(zb, yb, c, own.at[k], f32)
+            return 0
+
+        lax.fori_loop(0, 8, keep, 0)
+
+        def across(k, _):
+            core_copy(k).wait_recv()
+            ys[k, 0:size] = (own[k, 0:size] + cr[t, k, 0:size].astype(f32)).astype(bf16)
+            y_copy(k).start()
+            return 0
+
+        lax.fori_loop(0, 4, across, 0)
+
+        def near(k, _):
+            core_copy(k).wait_recv()
+            own[k, 0:size] = own[k, 0:size] + cr[t, k, 0:size].astype(f32)
+            return 0
+
+        lax.fori_loop(4, 8, near, 0)
+
+        def along(j, _):
+            k = j % Z
+            zb = (z + k) % Z
+            y_copy(zb).wait_recv()
+            value = own[4 + zb, 0:size] + yr[t, zb, 0:size].astype(f32)
+
+            @pl.when(k != 0)
+            def _():
+                zs[k, 0:size] = value.astype(bf16)
+                z_copy(k).start()
+
+            @pl.when(k == 0)
+            def _():
+                own[0, 0:size] = value
+
+            return 0
+
+        lax.fori_loop(1, Z + 1, along, 0)
+
+        def collect(k, total):
+            z_copy(k).wait_recv()
+            return total + zr[t, k, 0:size].astype(f32)
+
+        total = lax.fori_loop(1, Z, collect, own[0, 0:size])
+
+        def drain(k, _):
+            core_copy(k).wait_send()
+            return 0
+
+        lax.fori_loop(0, 8, drain, 0)
+
+        def drain_y(k, _):
+            y_copy(k).wait_send()
+            return 0
+
+        lax.fori_loop(0, 4, drain_y, 0)
+
+        def drain_z(k, _):
+            z_copy(k).wait_send()
+            return 0
+
+        lax.fori_loop(1, Z, drain_z, 0)
+        return total
+
+    def squares_of(values):
+        wide = values.astype(f32)
+        column = jnp.sum(wide * wide, axis=1, keepdims=True)
+        return jnp.broadcast_to(column_to_row(column), (8, rows))
+
+    def inverse(total):
+        return lax.rsqrt(total / D + 1e-05)
+
+    squares_start(steps, sqe_ref[...])
+
+    def united_block(zb, yb, cb, dst, kind):
+        at = pl.multiple_of((zb * 4 + yb * 2 + cb) * width, 128)
+        dst[...] = partial_ref[:, pl.ds(at, width)].astype(kind)
+
+    united = reduce_scatter(
+        steps, 0, rows, united_block, uown_ref, ucs_ref, ucr_ref, uys_ref, uyr_ref, uzs_ref, uzr_ref
+    ).astype(bf16)
+    h_ref[...] = united
+    inve_ref[...] = inverse(squares_total(steps))
+    squares_start(0, squares_of(united))
+
+    eye = (
+        lax.broadcasted_iota(jnp.int32, (rows, rows), 0)
+        == lax.broadcasted_iota(jnp.int32, (rows, rows), 1)
+    ).astype(f32)
+
+    def rope(values, cosine, sine):
+        return values * cosine + pltpu.roll(values, HD // 2, 1) * sine
+
+    def project(e, hg, at, size):
+        pe = jnp.dot(e, we_ref[:, pl.ds(at, size)], preferred_element_type=f32)
+        ph = jnp.dot(hg, wh_ref[:, pl.ds(at, size)], preferred_element_type=f32)
+        return pe, ph
+
+    def kv_copy(slot, base, source, k):
+        return remote(
+            kv_ref.at[pl.ds(base + source * quarter, quarter)],
+            kv_ref.at[pl.ds(base + source * quarter, quarter)],
+            kvs_sem.at[slot, k],
+            kvr_sem.at[slot, source],
+            z * 4 + (yc + k) % 4,
+        )
+
+    def kv_put(slot, base, values, table):
+        off = pl.multiple_of(yc * quarter, 8)
+        cosine = cos_ref[table, pl.ds(off, quarter), :]
+        sine = sin_ref[table, pl.ds(off, quarter), :]
+        where = pl.ds(pl.multiple_of(base + yc * quarter, quarter), quarter)
+        kv_ref[where, 0:HD] = rope(values[:, 0:HD], cosine, sine).astype(bf16)
+        kv_ref[where, HD : 2 * HD] = values[:, HD : 2 * HD].astype(bf16)
+        for k in range(1, 4):
+            kv_copy(slot, base, yc, k).start()
+
+    def kv_get(slot, base):
+        for k in range(1, 4):
+            kv_copy(slot, base, (yc + k) % 4, k).wait_recv()
+            kv_copy(slot, base, yc, k).wait_send()
+
+    def gather_copy(t, k, source, peer):
+        return remote(
+            att_ref.at[t, source], att_ref.at[t, source], ags_sem.at[t, k],
+            agr_sem.at[t, source], peer,
+        )
+
+    def step(t, first):
+        pick = pick_ref[t]
+        h_in = jnp.dot(pick, h_ref[...], preferred_element_type=f32).astype(bf16)
+        gain = gh_ref[0:1, :].astype(f32)
+        hg = (h_in.astype(f32) * gain).astype(bf16)
+        hg_ref[...] = hg
+        eg = eg_ref[t]
+        inv = inverse(squares_total(t))[0:1]
+        inv_h = row_to_column(pick, inv)
+        row_pick = (lax.broadcasted_iota(jnp.int32, (8, rows), 0) == t).astype(f32)
+        inv_e = row_to_column(eye, jnp.sum(inve_ref[...] * row_pick, axis=0, keepdims=True))
+        for half in range(2):
+            pe, ph = project(eg, hg, qcols + half * kcols, kcols)
+            kvp_ref[0, :, half * kcols : (half + 1) * kcols] = pe * inv_e + ph * inv_h
+        if first:
+            inv_u = row_to_column(eye, inv)
+            inv_v = row_to_column(eye, inve_ref[steps : steps + 1, :])
+            ug = (h_ref[...].astype(f32) * gain).astype(bf16)
+            for half in range(2):
+                pe, ph = project(eg_ref[steps], ug, qcols + half * kcols, kcols)
+                kvp_ref[1, :, half * kcols : (half + 1) * kcols] = pe * inv_v + ph * inv_u
+
+        def block(zb, yb, cb, dst, kind):
+            b = zb * 4 + yb * 2 + cb
+            pe, ph = project(
+                eg_ref[t], hg_ref[...], pl.multiple_of(b * block_cols, 128), block_cols
+            )
+            dst[0:rows, :] = (pe * inv_e + ph * inv_h).astype(kind)
+            off = pl.multiple_of((yb * 2 + cb) * quarter, 8)
+            for which in range(2 if first else 1):
+                for half in range(2):
+                    at = pl.multiple_of(half * kcols + zb * HD, 128)
+                    dst[
+                        rows + which * quarter : rows + (which + 1) * quarter,
+                        half * HD : (half + 1) * HD,
+                    ] = kvp_ref[which, pl.ds(off, quarter), pl.ds(at, HD)].astype(kind)
+
+        size = rows + (2 if first else 1) * quarter
+        total = reduce_scatter(
+            t, t, size, block, own_ref, cs_ref, cr_ref, ys_ref, yr_ref, zs_ref, zr_ref
+        )
+        sum_ref[0:size] = total
+        base = rows + t * rows
+        kv_put(t, base, sum_ref[rows : rows + quarter], t)
+        if first:
+            kv_put(steps, 0, sum_ref[rows + quarter : rows + 2 * quarter], steps)
+        cosine, sine = cos_ref[t], sin_ref[t]
+        queries = [
+            rope(sum_ref[0:rows, j * HD : (j + 1) * HD], cosine, sine).astype(bf16)
+            for j in range(block_cols // HD)
+        ]
+        kv_get(t, base)
+        if first:
+            kv_get(steps, 0)
+        allowed = mask_ref[t] > 0
+        keys = kv_ref[:, 0:HD]
+        vals = kv_ref[:, HD : 2 * HD]
+        for j, query in enumerate(queries):
+            scores = lax.dot_general(
+                query, keys, (((1,), (1,)), ((), ())), preferred_element_type=f32
+            ) / math.sqrt(HD)
+            scores = jnp.where(allowed, scores, MASKED)
+            expo = jnp.exp(scores - jnp.max(scores, axis=1, keepdims=True))
+            weights = (expo / jnp.sum(expo, axis=1, keepdims=True)).astype(bf16)
+            att_ref[t, me, :, j * HD : (j + 1) * HD] = jnp.dot(
+                weights, vals, preferred_element_type=f32
+            ).astype(bf16)
+
+        for k in range(1, Z):
+            gather_copy(t, k, me, ((z + k) % Z) * 4 + yc).start()
+        gather_copy(t, 4, me, y_peer).start()
+        gather_copy(t, 8, me, sibling).start()
+
+        def product(source):
+            at = pl.multiple_of(source * block_cols, 128)
+            return jnp.dot(
+                att_ref[t, source], wo_ref[pl.ds(at, block_cols), :], preferred_element_type=f32
+            )
+
+        part_ref[...] = h_in.astype(f32) + product(me)
+        for k in range(1, Z):
+            source = ((z + k) % Z) * 4 + yc
+            gather_copy(t, k, source, source).wait_recv()
+            gather_copy(t, 4 + k, source, y_peer).start()
+            gather_copy(t, 8 + k, source, sibling).start()
+            part_ref[...] += product(source)
+        for k in range(Z):
+            source = ((z + k) % Z) * 4 + (1 - y) * 2 + c
+            gather_copy(t, 4 + k, source, y_peer).wait_recv()
+            gather_copy(t, 12 + k, source, sibling).start()
+            part_ref[...] += product(source)
+        for yk in range(2):
+            for k in range(Z):
+                source = ((z + k) % Z) * 4 + ((y + yk) % 2) * 2 + (1 - c)
+                gather_copy(t, 8 + 4 * yk + k, source, sibling).wait_recv()
+                part_ref[...] += product(source)
+        for k in range(1, 16):
+            gather_copy(t, k, me, sibling).wait_send()
+        h_out = part_ref[...].astype(bf16)
+        h_ref[...] = h_out
+        out_ref[pl.ds(pl.multiple_of(t * rows, 128), rows), :] = h_out
+        return h_out
+
+    h_out = step(0, True)
+
+    def later(t, _):
+        squares_start(t, squares_of(h_ref[...]))
+        step(t, False)
+        return 0
+
+    lax.fori_loop(1, steps, later, 0)
+
+
+def local_kernel(
+    feats,
+    uniting_weight,
+    embeds_verified,
+    draft_embeds,
+    gain_embed,
+    gain_hidden,
+    proj_embed,
+    proj_hidden,
+    out_proj,
+    lengths,
+    root_seq,
+    parents,
+):
+    rows = feats.shape[0]
+    steps = draft_embeds.shape[0]
+    width = out_proj.shape[1]
+    qcols = out_proj.shape[0]
+    kcols = (proj_embed.shape[1] - qcols) // 2
+    block_cols = qcols // N
+    f32, bf16 = jnp.float32, jnp.bfloat16
+    ends = jnp.cumsum(lengths)
+    starts = ends - lengths
+    ids = jnp.arange(rows, dtype=jnp.int32)
+    slots = jnp.arange(lengths.shape[0], dtype=jnp.int32)
+    seg = jnp.sum((ids[:, None] >= ends[None, :]).astype(jnp.int32), axis=1)
+    of_seg = seg[:, None] == slots[None, :]
+    pos_v = ids - jnp.sum(jnp.where(of_seg, starts[None, :], 0), axis=1)
+
+    def look(table, index, count):
+        hit = index[:, None] == jnp.arange(count, dtype=jnp.int32)[None, :]
+        return jnp.sum(jnp.where(hit, table[None, :], 0), axis=1)
+
+    seq = root_seq
+    picks, masks, positions = [], [], []
+    ancestors = []
+    none = jnp.zeros((rows, rows), jnp.bool_)
+    for t in range(steps):
+        if t == 0:
+            link = look(ends - 1, root_seq, lengths.shape[0])
+        else:
+            link = parents[t - 1]
+            seq = look(seq, link, rows)
+            ancestors = [look(older, link, rows) for older in ancestors] + [link]
+        picks.append(link[:, None] == ids[None, :])
+        positions.append(look(lengths, seq, lengths.shape[0]) + t)
+        mask = [seg[None, :] == seq[:, None]]
+        mask += [older[:, None] == ids[None, :] for older in ancestors]
+        mask.append(ids[:, None] == ids[None, :])
+        mask += [none] * (steps + 1 - len(mask))
+        masks.append(jnp.concatenate(mask, axis=1))
+    positions.append(pos_v)
+    pick = jnp.stack(picks).astype(bf16)
+    mask = jnp.stack(masks).astype(f32)
+    half = HD // 2
+    freq = 500000.0 ** (-(jnp.arange(half, dtype=f32) * 2.0 / HD))
+    angle = jnp.stack(positions).astype(f32)[:, :, None] * freq[None, None, :]
+    cosine, sine = jnp.cos(angle), jnp.sin(angle)
+    cosine = jnp.concatenate([cosine, cosine], axis=-1)
+    sine = jnp.concatenate([-sine, sine], axis=-1)
+    embeds = jnp.concatenate([draft_embeds, embeds_verified[None]], axis=0)
+    wide = embeds.astype(f32)
+    eg = (wide * gain_embed.astype(f32)[None, None, :]).astype(bf16)
+    sqe = jnp.sum(wide * wide, axis=-1)
+    sqe = jnp.concatenate([sqe, jnp.zeros((8 - steps - 1, rows), f32)], axis=0)
+    gh = jnp.broadcast_to(gain_hidden[None, :], (16, width))
+    partial_value = jnp.dot(feats, uniting_weight, preferred_element_type=f32)
+    tall = rows + rows // 2
+    vmem = pl.BlockSpec(memory_space=pltpu.VMEM)
+    dma = pltpu.SemaphoreType.DMA
+    columns = pl.pallas_call(
+        functools.partial(draft_kernel, steps),
+        out_shape=jax.ShapeDtypeStruct((steps * rows, width), bf16),
+        in_specs=[vmem] * 11,
+        out_specs=vmem,
+        scratch_shapes=[
+            pltpu.VMEM((rows, width), bf16),
+            pltpu.VMEM((rows, width), bf16),
+            pltpu.VMEM((rows, width), f32),
+            pltpu.VMEM((2, rows, 2 * kcols), f32),
+            pltpu.VMEM((8, tall, block_cols), f32),
+            pltpu.VMEM((8, tall, block_cols), bf16),
+            pltpu.VMEM((steps, 8, tall, block_cols), bf16),
+            pltpu.VMEM((4, tall, block_cols), bf16),
+            pltpu.VMEM((steps, 4, tall, block_cols), bf16),
+            pltpu.VMEM((4, tall, block_cols), bf16),
+            pltpu.VMEM((steps, 4, tall, block_cols), bf16),
+            pltpu.VMEM((8, rows, width), f32),
+            pltpu.VMEM((8, rows, width), bf16),
+            pltpu.VMEM((1, 8, rows, width), bf16),
+            pltpu.VMEM((4, rows, width), bf16),
+            pltpu.VMEM((1, 4, rows, width), bf16),
+            pltpu.VMEM((4, rows, width), bf16),
+            pltpu.VMEM((1, 4, rows, width), bf16),
+            pltpu.VMEM((steps + 1, 8, rows), f32),
+            pltpu.VMEM((steps + 1, N, 8, rows), f32),
+            pltpu.VMEM(((steps + 1) * rows, 2 * HD), bf16),
+            pltpu.VMEM((steps, N, rows, block_cols), bf16),
+            pltpu.VMEM((tall, block_cols), f32),
+            pltpu.VMEM((8, rows), f32),
+            dma((steps + 1, 8)),
+            dma((steps + 1, 8)),
+            dma((steps + 1, 4)),
+            dma((steps + 1, 4)),
+            dma((steps + 1, 4)),
+            dma((steps + 1, 4)),
+            dma((steps + 1, N)),
+            dma((steps + 1, N)),
+            dma((steps + 1, 4)),
+            dma((steps + 1, 4)),
+            dma((steps, N)),
+            dma((steps, N)),
+        ],
+        compiler_params=pltpu.CompilerParams(
+            collective_id=0, has_side_effects=True, vmem_limit_bytes=60 * 1024 * 1024
+        ),
+    )(partial_value, eg, sqe, gh, proj_embed, proj_hidden, out_proj, pick, mask, cosine, sine)
+    return lax.all_to_all(columns, "section", split_axis=0, concat_axis=1, tiled=True)
+
+
 def solution(mesh):
     return jax.shard_map(
-        local,
+        local_kernel if mesh.shape["section"] == N else local_plain,
         mesh=mesh,
         in_specs=(
             P("groups", "section"),

time: 769 us -> 261 us (0.34); the launches traced: 758 us -> 258 us
  waiting for transfers between devices: 385 us -> 0 us
  Pallas kernels: 0 us -> 209 us
  blocking collectives: 136 us -> 19.1 us
  other arithmetic: 90.1 us -> 12.2 us
  local copies, waits for them, and re-layouts: 68.1 us -> 3.68 us
  matrix products: 62.8 us -> 13.5 us
  between operations: 15 us -> 0.16 us
    psum x4 -> x0, waiting for transfers between devices: 334 us -> none  [project_rows(): lax.psum(part_e * inv_e[:, None] + part_h * inv_h[:, None], 'section')]
    pallas_call x0 -> x1, Pallas kernels: none -> 209 us  [local_kernel(): pl.pallas_call(functools.partial(draft_kernel, steps), out_shape=jax.Shap...]
    psum x4 -> x0, blocking collectives: 116 us -> none  [project_rows(): total_e, total_h = lax.psum((square_e, square_h), 'section')]
    reduce_scatter x1 -> x0, waiting for transfers between devices: 50.6 us -> none  [local(): lax.psum_scatter(partial_value, 'section', scatter_dimension=1, tiled=True)]
    convert_element_type x7 -> x4, other arithmetic: 50.5 us -> 2.5 us  [the longest x1 1.15 us: local_kernel(): mask = jnp.stack(masks).astype(f32)]
    dot_general x22 -> x1, matrix products: 54 us -> 13.5 us  [local_kernel(): partial_value = jnp.dot(feats, uniting_weight, preferred_element_type=f32)]
    unnamed x162 -> x4, local copies, waits for them, and re-layouts: 24.5 us -> 0.01 us
    slice x19 -> x1, local copies, waits for them, and re-layouts: 17.6 us -> 0.8 us  [local_kernel(): link = parents[t - 1]]
  transfers between devices with their start and end apart: 5 -> 0, of which waited for: 5 -> 0; matrix products, arithmetic and copies ran while one was open for 11% -> 0% of each run, Pallas kernels for 0% -> 0%
where the time goes in v1:
time: 261 us; the launch traced here: 258 us
  Pallas kernels  209 us (80%)
  blocking collectives  19.1 us (7%)
  matrix products  13.5 us (5%)
  other arithmetic  12.2 us (5%)
  local copies, waits for them, and re-layouts  3.68 us (1%)
    pallas_call x1, Pallas kernels, local_kernel(): pl.pallas_call(functools.partial(draft_kernel, steps), out_shape=jax.Shap...  209 us
    all_to_all x1, blocking collectives, local_kernel(): lax.all_to_all(columns, 'section', split_axis=0, concat_axis=1, tiled=True)  19.1 us
    dot_general x1, matrix products, local_kernel(): partial_value = jnp.dot(feats, uniting_weight, preferred_element_type=f32)  13.5 us

profile of v1, /device:TPU:31, one launch (start us, length us, event | category | flops | bytes accessed | tf_op | source)
XLA Modules:
  0.0 257.7 jit_solution(16253256533814808472)
XLA Ops:
  0.0 0.8 copy.17
  0.8 0.1 reduce
  1.0 0.1 convert_reduce_fusion
  1.0 0.7 fusion.10
  1.7 0.8 slice_bitcast_fusion.2
  2.5 0.1 iota_compare_fusion.9
  2.6 0.1 iota_compare_fusion.5
  2.7 0.8 select_reduce_fusion.5
  3.6 0.7 convert_element_type.26
  4.3 0.2 select_reduce_fusion.3
  4.4 0.1 iota_compare_fusion.7
  4.5 0.2 select_reduce_fusion
  4.8 0.8 broadcast_compare_fusion.1
  5.6 0.8 select_reduce_fusion.7
  6.4 0.1 iota_compare_fusion.10
  6.5 0.1 fusion.5
  6.6 0.1 fusion.6
  6.7 0.1 fusion.7
  6.8 0.1 fusion.3
  7.0 1.2 fusion.2
  8.2 0.9 pad_maximum_fusion.1.cos_ref
  9.1 2.2 fusion.1
  11.3 0.6 concatenate.35.sqe_ref
  11.9 0.9 pad_maximum_fusion.2.sin_ref
  12.7 13.5 %fusion.11.partial_ref = f32[128,8192]{1,0:T(8,128)} fusion(bf16[128,1536]{1,0:T(8,128)(2,1)S(1)} %copy-done, bf16[1536,8192]{1,0:T(8,128)(2,1)} %param.13), kind=kOutput, calls=%fused_computation.66 | convolution fusion | flops 3221225472 | bytes 29753344 | tf_op jit(solution)/shard_map/dot_general | solution.py:629
  26.3 0.7 add_convert_fusion.1.pick_ref
  26.9 0.1 add_bitcast_fusion
  27.0 1.1 add_convert_fusion.mask_ref
  28.2 0.6 broadcast_in_dim.85.gh_ref
  28.8 209.0 %shard_map.118 = bf16[512,512]{1,0:T(8,128)(2,1)} custom-call(f32[128,8192]{1,0:T(8,128)} %fusion.11.partial_ref, bf16[5,128,512]{2,1,0:T(8,128)(2,1)} %get-tuple-element.16.eg_ref, f32[8,128]{1,0:T(8,128)} %concatenate.35.sqe_ref, bf16[16,512]{1,0:T(8,128)(2,1)} %broadcast_in_dim.85.gh_ref, bf16[512,5120]{1,0:T(8,128)(2,1)} %we_ref.1, ...), custom_call_target="tpu_custom_call" | custom-call | tf_op jit(solution)/shard_map/pallas_call | solution.py:633
  237.8 19.1 %all_to_all.19 = bf16[16,32,512]{2,1,0:T(8,128)(2,1)S(1)} all-to-all(bf16[16,32,512]{2,1,0:T(8,128)(2,1)} %bitcast.30), channel_id=1, replica_groups=mesh['groups'=2,'section'=16] {'section'}, dimensions={0} | all-to-all | bytes 1048576 | tf_op jit(solution)/shard_map/all_to_all | solution.py:680
  256.8 0.8 copy.19
  (19 shorter events, 0.2 us)
Async XLA Ops:
  0.0 12.7 %copy-start = (bf16[128,1536]{1,0:T(8,128)(2,1)S(1)}, bf16[128,1536]{1,0:T(8,128)(2,1)}, u32[]{:S(2)}) copy-start(bf16[128,1536]{1,0:T(8,128)(2,1)} %param.12) | copy-start | bytes 1179652
  12.7 15.4 %copy-start.1 = (bf16[512]{0:T(512)(128)(2,1)S(1)}, bf16[512]{0:T(512)(128)(2,1)}, u32[]{:S(2)}) copy-start(bf16[512]{0:T(512)(128)(2,1)} %param.17) | copy-start | bytes 3076

commit v2 on v1

--- a/solution.py
+++ b/solution.py
@@ -177,18 +177,31 @@
 
 def draft_kernel(
     steps,
-    partial_ref,
+    feats_ref,
+    uniting_ref,
     eg_ref,
     sqe_ref,
     gh_ref,
-    we_ref,
-    wh_ref,
-    wo_ref,
+    we_hbm,
+    wh_hbm,
+    wo_hbm,
     pick_ref,
     mask_ref,
     cos_ref,
     sin_ref,
     out_ref,
+    we_ref,
+    wh_ref,
+    wo_ref,
+    strip_ref,
+    pe_ref,
+    ctx_ref,
+    hist_ref,
+    rows_ref,
+    strip_sem,
+    weight_sem,
+    outs_sem,
+    outr_sem,
     h_ref,
     hg_ref,
     part_ref,
@@ -285,10 +298,10 @@
 
         return lax.fori_loop(1, N, go, sqr_ref[slot, me])
 
-    def reduce_scatter(s, t, size, block, own, cs, cr, ys, yr, zs, zr):
+    def reduce_scatter(s, t, size, block, own, cs, cr, ys, yr, zs, zr, meanwhile=None):
         def order(k):
             far = k < 4
-            return jnp.where(far, k, k - 4), jnp.where(far, 1 - y, y)
+            return (z + 1 + jnp.where(far, k, k - 4)) % Z, jnp.where(far, 1 - y, y)
 
         def core_copy(k):
             return remote(
@@ -303,66 +316,63 @@
             )
 
         def z_copy(k):
-            other = (z + k) % Z
             return remote(
                 zs.at[k, pl.ds(0, size)], zr.at[t, k, pl.ds(0, size)], zs_sem.at[s, k],
-                zr_sem.at[s, k], other * 4 + yc,
+                zr_sem.at[s, k], ((z + 1 + k) % Z) * 4 + yc,
             )
 
         def give(k, _):
             zb, yb = order(k)
-            block(zb, yb, 1 - c, cs.at[k], bf16)
+            block(zb, yb, 1 - c, cs.at[k], bf16, k + jnp.where(k < 4, 0, 4))
             core_copy(k).start()
             return 0
 
-        lax.fori_loop(0, 8, give, 0)
-
         def keep(k, _):
             zb, yb = order(k)
-            block(zb, yb, c, own.at[k], f32)
+            block(zb, yb, c, own.at[k], f32, k + jnp.where(k < 4, 4, 8))
             return 0
 
-        lax.fori_loop(0, 8, keep, 0)
-
         def across(k, _):
+            keep(k, 0)
             core_copy(k).wait_recv()
             ys[k, 0:size] = (own[k, 0:size] + cr[t, k, 0:size].astype(f32)).astype(bf16)
             y_copy(k).start()
             return 0
 
+        lax.fori_loop(0, 4, give, 0)
         lax.fori_loop(0, 4, across, 0)
-
-        def near(k, _):
-            core_copy(k).wait_recv()
-            own[k, 0:size] = own[k, 0:size] + cr[t, k, 0:size].astype(f32)
-            return 0
-
-        lax.fori_loop(4, 8, near, 0)
-
-        def along(j, _):
-            k = j % Z
-            zb = (z + k) % Z
-            y_copy(zb).wait_recv()
-            value = own[4 + zb, 0:size] + yr[t, zb, 0:size].astype(f32)
-
-            @pl.when(k != 0)
+        lax.fori_loop(4, 8, give, 0)
+        lax.fori_loop(4, 8, keep, 0)
+
+        def along(k, _):
+            core_copy(k + 4).wait_recv()
+            y_copy(k).wait_recv()
+            value = (
+                own[4 + k, 0:size]
+                + cr[t, 4 + k, 0:size].astype(f32)
+                + yr[t, k, 0:size].astype(f32)
+            )
+
+            @pl.when(k < Z - 1)
             def _():
                 zs[k, 0:size] = value.astype(bf16)
                 z_copy(k).start()
 
-            @pl.when(k == 0)
+            @pl.when(k == Z - 1)
             def _():
                 own[0, 0:size] = value
 
             return 0
 
-        lax.fori_loop(1, Z + 1, along, 0)
+        lax.fori_loop(0, Z, along, 0)
+        if meanwhile is not None:
+            meanwhile()
 
         def collect(k, total):
             z_copy(k).wait_recv()
             return total + zr[t, k, 0:size].astype(f32)
 
-        total = lax.fori_loop(1, Z, collect, own[0, 0:size])
+        total = lax.fori_loop(0, Z - 1, collect, own[0, 0:size])
 
         def drain(k, _):
             core_copy(k).wait_send()
@@ -380,7 +390,7 @@
             z_copy(k).wait_send()
             return 0
 
-        lax.fori_loop(1, Z, drain_z, 0)
+        lax.fori_loop(0, Z - 1, drain_z, 0)
         return total
 
     def squares_of(values):
@@ -393,29 +403,85 @@
 
     squares_start(steps, sqe_ref[...])
 
-    def united_block(zb, yb, cb, dst, kind):
-        at = pl.multiple_of((zb * 4 + yb * 2 + cb) * width, 128)
-        dst[...] = partial_ref[:, pl.ds(at, width)].astype(kind)
-
-    united = reduce_scatter(
-        steps, 0, rows, united_block, uown_ref, ucs_ref, ucr_ref, uys_ref, uyr_ref, uzs_ref, uzr_ref
-    ).astype(bf16)
-    h_ref[...] = united
-    inve_ref[...] = inverse(squares_total(steps))
-    squares_start(0, squares_of(united))
-
     eye = (
         lax.broadcasted_iota(jnp.int32, (rows, rows), 0)
         == lax.broadcasted_iota(jnp.int32, (rows, rows), 1)
     ).astype(f32)
 
+    depth = strip_ref.shape[0]
+
+    def strip(n):
+        second = n // 4 % 2
+        zb = (z + 1 + n % 4) % Z
+        yb = jnp.where(n < 8, 1 - y, y)
+        cb = jnp.where(second == 0, 1 - c, c)
+        at = pl.multiple_of((zb * 4 + yb * 2 + cb) * width, 128)
+        return pltpu.make_async_copy(
+            uniting_ref.at[:, pl.ds(at, width)], strip_ref.at[n % depth], strip_sem.at[n % depth]
+        )
+
+    weights = [
+        pltpu.make_async_copy(src, dst, weight_sem.at[i])
+        for i, (src, dst) in enumerate(
+            ((we_hbm, we_ref), (wh_hbm, wh_ref), (wo_hbm, wo_ref))
+        )
+    ]
+
+    def united_block(zb, yb, cb, dst, kind, n):
+        strip(n).wait()
+        dst[...] = jnp.dot(
+            feats_ref[...], strip_ref[n % depth], preferred_element_type=f32
+        ).astype(kind)
+
+        @pl.when(n + depth < N)
+        def _():
+            strip(n + depth).start()
+
+    def embed_products():
+        for copy in weights:
+            copy.wait()
+        inve_ref[...] = inverse(squares_total(steps))
+        columns = [row_to_column(eye, inve_ref[t : t + 1, :]) for t in range(steps + 1)]
+        tall = jnp.concatenate(columns[:steps], axis=0)
+
+        def go(i, _):
+            at = pl.multiple_of(i * block_cols, 128)
+            pe_ref[i] = (
+                jnp.dot(
+                    eg_ref[0 : steps * rows, :],
+                    we_ref[:, pl.ds(at, block_cols)],
+                    preferred_element_type=f32,
+                )
+                * tall
+            )
+            return 0
+
+        lax.fori_loop(0, pe_ref.shape[0], go, 0)
+        ctx_ref[...] = (
+            jnp.dot(
+                eg_ref[steps * rows : (steps + 1) * rows, :],
+                we_ref[:, qcols:],
+                preferred_element_type=f32,
+            )
+            * columns[steps]
+        )
+
+    for n in range(depth):
+        strip(n).start()
+    for copy in weights:
+        copy.start()
+    united = reduce_scatter(
+        steps, 0, rows, united_block, uown_ref, ucs_ref, ucr_ref, uys_ref, uyr_ref, uzs_ref,
+        uzr_ref, embed_products,
+    ).astype(bf16)
+    h_ref[...] = united
+    squares_start(0, squares_of(united))
+
     def rope(values, cosine, sine):
         return values * cosine + pltpu.roll(values, HD // 2, 1) * sine
 
-    def project(e, hg, at, size):
-        pe = jnp.dot(e, we_ref[:, pl.ds(at, size)], preferred_element_type=f32)
-        ph = jnp.dot(hg, wh_ref[:, pl.ds(at, size)], preferred_element_type=f32)
-        return pe, ph
+    def project(hg, at, size):
+        return jnp.dot(hg, wh_ref[:, pl.ds(at, size)], preferred_element_type=f32)
 
     def kv_copy(slot, base, source, k):
         return remote(
@@ -453,28 +519,28 @@
         gain = gh_ref[0:1, :].astype(f32)
         hg = (h_in.astype(f32) * gain).astype(bf16)
         hg_ref[...] = hg
-        eg = eg_ref[t]
         inv = inverse(squares_total(t))[0:1]
         inv_h = row_to_column(pick, inv)
-        row_pick = (lax.broadcasted_iota(jnp.int32, (8, rows), 0) == t).astype(f32)
-        inv_e = row_to_column(eye, jnp.sum(inve_ref[...] * row_pick, axis=0, keepdims=True))
-        for half in range(2):
-            pe, ph = project(eg, hg, qcols + half * kcols, kcols)
-            kvp_ref[0, :, half * kcols : (half + 1) * kcols] = pe * inv_e + ph * inv_h
+        own_rows = pl.ds(pl.multiple_of(t * rows, 128), rows)
+        pairs = 2 * kcols // block_cols
+        for i in range(pairs):
+            at = i * block_cols
+            kvp_ref[0, :, at : at + block_cols] = (
+                pe_ref[N + i, own_rows] + project(hg, qcols + at, block_cols) * inv_h
+            )
         if first:
             inv_u = row_to_column(eye, inv)
-            inv_v = row_to_column(eye, inve_ref[steps : steps + 1, :])
             ug = (h_ref[...].astype(f32) * gain).astype(bf16)
-            for half in range(2):
-                pe, ph = project(eg_ref[steps], ug, qcols + half * kcols, kcols)
-                kvp_ref[1, :, half * kcols : (half + 1) * kcols] = pe * inv_v + ph * inv_u
-
-        def block(zb, yb, cb, dst, kind):
+            for i in range(pairs):
+                at = i * block_cols
+                kvp_ref[1, :, at : at + block_cols] = (
+                    ctx_ref[:, at : at + block_cols] + project(ug, qcols + at, block_cols) * inv_u
+                )
+
+        def block(zb, yb, cb, dst, kind, n):
             b = zb * 4 + yb * 2 + cb
-            pe, ph = project(
-                eg_ref[t], hg_ref[...], pl.multiple_of(b * block_cols, 128), block_cols
-            )
-            dst[0:rows, :] = (pe * inv_e + ph * inv_h).astype(kind)
+            ph = project(hg_ref[...], pl.multiple_of(b * block_cols, 128), block_cols)
+            dst[0:rows, :] = (pe_ref[b, own_rows] + ph * inv_h).astype(kind)
             off = pl.multiple_of((yb * 2 + cb) * quarter, 8)
             for which in range(2 if first else 1):
                 for half in range(2):
@@ -501,19 +567,22 @@
         kv_get(t, base)
         if first:
             kv_get(steps, 0)
-        allowed = mask_ref[t] > 0
         keys = kv_ref[:, 0:HD]
         vals = kv_ref[:, HD : 2 * HD]
-        for j, query in enumerate(queries):
-            scores = lax.dot_general(
-                query, keys, (((1,), (1,)), ((), ())), preferred_element_type=f32
-            ) / math.sqrt(HD)
-            scores = jnp.where(allowed, scores, MASKED)
-            expo = jnp.exp(scores - jnp.max(scores, axis=1, keepdims=True))
-            weights = (expo / jnp.sum(expo, axis=1, keepdims=True)).astype(bf16)
-            att_ref[t, me, :, j * HD : (j + 1) * HD] = jnp.dot(
-                weights, vals, preferred_element_type=f32
-            ).astype(bf16)
+        heads = len(queries)
+        allowed = jnp.concatenate([mask_ref[t]] * heads, axis=0) > 0
+        scores = lax.dot_general(
+            jnp.concatenate(queries, axis=0),
+            keys,
+            (((1,), (1,)), ((), ())),
+            preferred_element_type=f32,
+        ) / math.sqrt(HD)
+        scores = jnp.where(allowed, scores, MASKED)
+        expo = jnp.exp(scores - jnp.max(scores, axis=1, keepdims=True))
+        weights = (expo / jnp.sum(expo, axis=1, keepdims=True)).astype(bf16)
+        mixed = jnp.dot(weights, vals, preferred_element_type=f32).astype(bf16)
+        for j in range(heads):
+            att_ref[t, me, :, j * HD : (j + 1) * HD] = mixed[j * rows : (j + 1) * rows]
 
         for k in range(1, Z):
             gather_copy(t, k, me, ((z + k) % Z) * 4 + yc).start()
@@ -547,10 +616,28 @@
             gather_copy(t, k, me, sibling).wait_send()
         h_out = part_ref[...].astype(bf16)
         h_ref[...] = h_out
-        out_ref[pl.ds(pl.multiple_of(t * rows, 128), rows), :] = h_out
-        return h_out
-
-    h_out = step(0, True)
+        hist_ref[t] = h_out
+        for q in range(4):
+            owner = t * 4 + q
+
+            @pl.when(owner != me)
+            def _():
+                out_copy(t, q, me).start()
+
+            @pl.when(owner == me)
+            def _():
+                rows_ref[me] = hist_ref[t, q * quarter : (q + 1) * quarter]
+
+    def out_copy(t, q, source):
+        return remote(
+            hist_ref.at[t, pl.ds(q * quarter, quarter)],
+            rows_ref.at[source],
+            outs_sem.at[t, q],
+            outr_sem.at[source],
+            t * 4 + q,
+        )
+
+    step(0, True)
 
     def later(t, _):
         squares_start(t, squares_of(h_ref[...]))
@@ -558,6 +645,23 @@
         return 0
 
     lax.fori_loop(1, steps, later, 0)
+
+    for t in range(steps):
+        for q in range(4):
+
+            @pl.when(t * 4 + q != me)
+            def _():
+                out_copy(t, q, me).wait_send()
+
+    out_ref[:, pl.ds(pl.multiple_of(me * width, 128), width)] = rows_ref[me]
+
+    def place(k, _):
+        source = (me + k) % N
+        out_copy(0, 0, source).wait_recv()
+        out_ref[:, pl.ds(pl.multiple_of(source * width, 128), width)] = rows_ref[source]
+        return 0
+
+    lax.fori_loop(1, N, place, 0)
 
 
 def local_kernel(
@@ -623,19 +727,32 @@
     embeds = jnp.concatenate([draft_embeds, embeds_verified[None]], axis=0)
     wide = embeds.astype(f32)
     eg = (wide * gain_embed.astype(f32)[None, None, :]).astype(bf16)
+    eg = eg.reshape((steps + 1) * rows, width)
     sqe = jnp.sum(wide * wide, axis=-1)
     sqe = jnp.concatenate([sqe, jnp.zeros((8 - steps - 1, rows), f32)], axis=0)
     gh = jnp.broadcast_to(gain_hidden[None, :], (16, width))
-    partial_value = jnp.dot(feats, uniting_weight, preferred_element_type=f32)
     tall = rows + rows // 2
     vmem = pl.BlockSpec(memory_space=pltpu.VMEM)
     dma = pltpu.SemaphoreType.DMA
-    columns = pl.pallas_call(
+    hbm = pl.BlockSpec(memory_space=pl.ANY)
+    return pl.pallas_call(
         functools.partial(draft_kernel, steps),
-        out_shape=jax.ShapeDtypeStruct((steps * rows, width), bf16),
-        in_specs=[vmem] * 11,
+        out_shape=jax.ShapeDtypeStruct((steps * rows // N, N * width), bf16),
+        in_specs=[vmem, hbm] + [vmem] * 3 + [hbm] * 3 + [vmem] * 4,
         out_specs=vmem,
         scratch_shapes=[
+            pltpu.VMEM(proj_embed.shape, bf16),
+            pltpu.VMEM(proj_hidden.shape, bf16),
+            pltpu.VMEM(out_proj.shape, bf16),
+            pltpu.VMEM((4, feats.shape[1], width), bf16),
+            pltpu.VMEM((proj_embed.shape[1] // block_cols, steps * rows, block_cols), f32),
+            pltpu.VMEM((rows, 2 * kcols), f32),
+            pltpu.VMEM((steps, rows, width), bf16),
+            pltpu.VMEM((N, rows // 4, width), bf16),
+            dma((4,)),
+            dma((3,)),
+            dma((steps, 4)),
+            dma((N,)),
             pltpu.VMEM((rows, width), bf16),
             pltpu.VMEM((rows, width), bf16),
             pltpu.VMEM((rows, width), f32),
@@ -676,8 +793,10 @@
         compiler_params=pltpu.CompilerParams(
             collective_id=0, has_side_effects=True, vmem_limit_bytes=60 * 1024 * 1024
         ),
-    )(partial_value, eg, sqe, gh, proj_embed, proj_hidden, out_proj, pick, mask, cosine, sine)
-    return lax.all_to_all(columns, "section", split_axis=0, concat_axis=1, tiled=True)
+    )(
+        feats, uniting_weight, eg, sqe, gh, proj_embed, proj_hidden, out_proj, pick, mask, cosine,
+        sine,
+    )
 
 
 def solution(mesh):

time: 261 us -> 220 us (0.84); the launches traced: 258 us -> 220 us
  blocking collectives: 19.1 us -> 0 us
  matrix products: 13.5 us -> 0 us
  other arithmetic: 12.2 us -> 9.2 us
    all_to_all x1 -> x0, blocking collectives: 19.1 us -> none  [local_kernel(): lax.all_to_all(columns, 'section', split_axis=0, concat_axis=1, tiled=True)]
    dot_general x1 -> x0, matrix products: 13.5 us -> none  [local_kernel(): partial_value = jnp.dot(feats, uniting_weight, preferred_element_type=f32)]
where the time goes in v2:
time: 220 us
  Pallas kernels  207 us (94%)
  other arithmetic  9.2 us (4%)
  local copies, waits for them, and re-layouts  3.25 us (1%)
    pallas_call x1, Pallas kernels, local_kernel(): pl.pallas_call(functools.partial(draft_kernel, steps), out_shape=jax.Shap...  207 us

profile of v2, /device:TPU:31, one launch (start us, length us, event | category | flops | bytes accessed | tf_op | source)
XLA Modules:
  0.0 219.7 jit_solution(3167949099265276973)
XLA Ops:
  0.0 1.2 maximum_convert_fusion
  1.2 0.0 copy-start
  1.3 0.0 copy-start.6
  1.3 0.0 copy-start.2
  1.3 1.0 fusion.eg_ref
  2.3 0.2 multiply_reduce_fusion
  2.5 0.6 concatenate.35.sqe_ref
  3.1 0.6 broadcast_in_dim.85.gh_ref
  3.7 0.1 iota_compare_fusion.7
  3.8 0.1 iota_compare_fusion.9
  3.9 0.2 select_reduce_fusion.5
  4.1 0.2 select_reduce_fusion.3
  4.3 0.2 select_reduce_fusion
  4.5 0.1 copy.15
  4.7 0.1 reduce
  4.8 0.1 convert_reduce_fusion
  4.9 0.1 select_reduce_fusion.7
  5.0 0.1 iota_compare_fusion.10
  5.1 0.7 add_convert_fusion.1.pick_ref
  5.7 0.1 broadcast_compare_fusion.1
  5.9 0.1 fusion.5
  6.0 0.1 fusion.6
  6.1 0.1 fusion.4
  6.2 0.1 fusion.2
  6.4 0.1 iota_compare_fusion.5
  6.5 0.1 add_bitcast_fusion
  6.6 1.2 add_convert_fusion.mask_ref
  7.8 1.2 fusion.1
  9.1 0.9 pad_maximum_fusion.cos_ref
  9.9 0.9 pad_maximum_fusion.1.sin_ref
  10.8 207.0 %shard_map.118 = bf16[32,8192]{1,0:T(8,128)(2,1)} custom-call(bf16[128,1536]{1,0:T(8,128)(2,1)} %feats_ref.1, bf16[1536,8192]{1,0:T(8,128)(2,1)} %uniting_ref.1, bf16[640,512]{1,0:T(8,128)(2,1)} %fusion.eg_ref, f32[8,128]{1,0:T(8,128)} %concatenate.35.sqe_ref, bf16[16,512]{1,0:T(8,128)(2,1)} %broadcast_in_dim.85.gh_ref, bf16[512,5120]{1,0:T(8,128)(2,1)} %we_hbm.1, ...), custom_call_target="tpu_custom_call" | custom-call | tf_op jit(solution)/shard_map/pallas_call | solution.py:738
  217.8 1.9 copy.25
  (29 shorter events, 0.2 us)
Async XLA Ops:
  0.0 1.2 copy-start.5
  1.2 1.1 copy-start
  1.2 1.1 copy-start.1
  1.3 1.9 copy-start.6
  1.3 2.5 %copy-start.4 = (s32[3,128]{1,0:T(4,128)S(1)}, s32[3,128]{1,0:T(4,128)}, u32[]{:S(2)}) copy-start(s32[3,128]{1,0:T(4,128)} %param.23) | copy-start | bytes 4612
  1.3 2.7 %copy-start.3 = (s32[128]{0:T(128)S(1)}, s32[128]{0:T(128)}, u32[]{:S(2)}) copy-start(s32[128]{0:T(128)} %param.22) | copy-start | bytes 1540
  1.3 3.2 %copy-start.2 = (s32[16]{0:T(128)S(1)}, s32[16]{0:T(128)}, u32[]{:S(2)}) copy-start(s32[16]{0:T(128)} %param.21) | copy-start | bytes 196

commit v3 on v2

--- a/solution.py
+++ b/solution.py
@@ -195,6 +195,7 @@
     wo_ref,
     strip_ref,
     pe_ref,
+    ph_ref,
     ctx_ref,
     hist_ref,
     rows_ref,
@@ -374,24 +375,24 @@
 
         total = lax.fori_loop(0, Z - 1, collect, own[0, 0:size])
 
-        def drain(k, _):
-            core_copy(k).wait_send()
-            return 0
-
-        lax.fori_loop(0, 8, drain, 0)
-
-        def drain_y(k, _):
-            y_copy(k).wait_send()
-            return 0
-
-        lax.fori_loop(0, 4, drain_y, 0)
-
-        def drain_z(k, _):
-            z_copy(k).wait_send()
-            return 0
-
-        lax.fori_loop(0, Z - 1, drain_z, 0)
-        return total
+        def drain():
+            def both(k, _):
+                core_copy(k).wait_send()
+                return 0
+
+            def cross(k, _):
+                y_copy(k).wait_send()
+                return 0
+
+            def deep(k, _):
+                z_copy(k).wait_send()
+                return 0
+
+            lax.fori_loop(0, 8, both, 0)
+            lax.fori_loop(0, 4, cross, 0)
+            lax.fori_loop(0, Z - 1, deep, 0)
+
+        return total, drain
 
     def squares_of(values):
         wide = values.astype(f32)
@@ -470,10 +471,11 @@
         strip(n).start()
     for copy in weights:
         copy.start()
-    united = reduce_scatter(
+    united, drain_united = reduce_scatter(
         steps, 0, rows, united_block, uown_ref, ucs_ref, ucr_ref, uys_ref, uyr_ref, uzs_ref,
         uzr_ref, embed_products,
-    ).astype(bf16)
+    )
+    united = united.astype(bf16)
     h_ref[...] = united
     squares_start(0, squares_of(united))
 
@@ -519,28 +521,28 @@
         gain = gh_ref[0:1, :].astype(f32)
         hg = (h_in.astype(f32) * gain).astype(bf16)
         hg_ref[...] = hg
+        pairs = 2 * kcols // block_cols
+
+        def raw(i, _):
+            ph_ref[i] = project(hg_ref[...], pl.multiple_of(i * block_cols, 128), block_cols)
+            return 0
+
+        lax.fori_loop(0, N + pairs, raw, 0, unroll=4)
+        if first:
+            ug = (h_ref[...].astype(f32) * gain).astype(bf16)
+            kvp_ref[1] = project(ug, qcols, 2 * kcols)
         inv = inverse(squares_total(t))[0:1]
         inv_h = row_to_column(pick, inv)
         own_rows = pl.ds(pl.multiple_of(t * rows, 128), rows)
-        pairs = 2 * kcols // block_cols
         for i in range(pairs):
             at = i * block_cols
-            kvp_ref[0, :, at : at + block_cols] = (
-                pe_ref[N + i, own_rows] + project(hg, qcols + at, block_cols) * inv_h
-            )
+            kvp_ref[0, :, at : at + block_cols] = pe_ref[N + i, own_rows] + ph_ref[N + i] * inv_h
         if first:
-            inv_u = row_to_column(eye, inv)
-            ug = (h_ref[...].astype(f32) * gain).astype(bf16)
-            for i in range(pairs):
-                at = i * block_cols
-                kvp_ref[1, :, at : at + block_cols] = (
-                    ctx_ref[:, at : at + block_cols] + project(ug, qcols + at, block_cols) * inv_u
-                )
+            kvp_ref[1] = ctx_ref[...] + kvp_ref[1] * row_to_column(eye, inv)
 
         def block(zb, yb, cb, dst, kind, n):
             b = zb * 4 + yb * 2 + cb
-            ph = project(hg_ref[...], pl.multiple_of(b * block_cols, 128), block_cols)
-            dst[0:rows, :] = (pe_ref[b, own_rows] + ph * inv_h).astype(kind)
+            dst[0:rows, :] = (pe_ref[b, own_rows] + ph_ref[b] * inv_h).astype(kind)
             off = pl.multiple_of((yb * 2 + cb) * quarter, 8)
             for which in range(2 if first else 1):
                 for half in range(2):
@@ -551,7 +553,7 @@
                     ] = kvp_ref[which, pl.ds(off, quarter), pl.ds(at, HD)].astype(kind)
 
         size = rows + (2 if first else 1) * quarter
-        total = reduce_scatter(
+        total, drain = reduce_scatter(
             t, t, size, block, own_ref, cs_ref, cr_ref, ys_ref, yr_ref, zs_ref, zr_ref
         )
         sum_ref[0:size] = total
@@ -612,10 +614,16 @@
                 source = ((z + k) % Z) * 4 + ((y + yk) % 2) * 2 + (1 - c)
                 gather_copy(t, 8 + 4 * yk + k, source, sibling).wait_recv()
                 part_ref[...] += product(source)
-        for k in range(1, 16):
-            gather_copy(t, k, me, sibling).wait_send()
         h_out = part_ref[...].astype(bf16)
         h_ref[...] = h_out
+        if first:
+            squares_start(1, squares_of(h_out))
+        else:
+
+            @pl.when(t < steps - 1)
+            def _():
+                squares_start(t + 1, squares_of(h_ref[...]))
+
         hist_ref[t] = h_out
         for q in range(4):
             owner = t * 4 + q
@@ -627,6 +635,12 @@
             @pl.when(owner == me)
             def _():
                 rows_ref[me] = hist_ref[t, q * quarter : (q + 1) * quarter]
+
+        drain()
+        for k in range(1, 16):
+            gather_copy(t, k, me, sibling).wait_send()
+        if first:
+            drain_united()
 
     def out_copy(t, q, source):
         return remote(
@@ -640,7 +654,6 @@
     step(0, True)
 
     def later(t, _):
-        squares_start(t, squares_of(h_ref[...]))
         step(t, False)
         return 0
 
@@ -744,12 +757,13 @@
             pltpu.VMEM(proj_embed.shape, bf16),
             pltpu.VMEM(proj_hidden.shape, bf16),
             pltpu.VMEM(out_proj.shape, bf16),
-            pltpu.VMEM((4, feats.shape[1], width), bf16),
+            pltpu.VMEM((3, feats.shape[1], width), bf16),
             pltpu.VMEM((proj_embed.shape[1] // block_cols, steps * rows, block_cols), f32),
+            pltpu.VMEM((proj_embed.shape[1] // block_cols, rows, block_cols), f32),
             pltpu.VMEM((rows, 2 * kcols), f32),
             pltpu.VMEM((steps, rows, width), bf16),
             pltpu.VMEM((N, rows // 4, width), bf16),
-            dma((4,)),
+            dma((3,)),
             dma((3,)),
             dma((steps, 4)),
             dma((N,)),

time: 220 us -> 208 us (0.945)
  Pallas kernels: 207 us -> 195 us
    pallas_call x1, Pallas kernels: 207 us -> 195 us  [local_kernel(): pl.pallas_call(functools.partial(draft_kernel, steps), out_shape=jax.Shap...]
where the time goes in v3:
time: 208 us
  Pallas kernels  195 us (94%)
  other arithmetic  9.2 us (4%)
  local copies, waits for them, and re-layouts  3.25 us (2%)
    pallas_call x1, Pallas kernels, local_kernel(): pl.pallas_call(functools.partial(draft_kernel, steps), out_shape=jax.Shap...  195 us

profile of v3, /device:TPU:31, one launch (start us, length us, event | category | flops | bytes accessed | tf_op | source)
XLA Modules:
  0.0 207.7 jit_solution(5822977940761585341)
XLA Ops:
  0.0 1.2 maximum_convert_fusion
  1.2 0.0 copy-start
  1.3 0.0 copy-start.6
  1.3 0.0 copy-start.2
  1.3 1.0 fusion.eg_ref
  2.3 0.2 multiply_reduce_fusion
  2.5 0.6 concatenate.35.sqe_ref
  3.1 0.6 broadcast_in_dim.85.gh_ref
  3.7 0.1 iota_compare_fusion.7
  3.8 0.1 iota_compare_fusion.9
  3.9 0.2 select_reduce_fusion.5
  4.1 0.2 select_reduce_fusion.3
  4.3 0.2 select_reduce_fusion
  4.5 0.1 copy.15
  4.7 0.1 reduce
  4.8 0.1 convert_reduce_fusion
  4.9 0.1 select_reduce_fusion.7
  5.0 0.1 iota_compare_fusion.10
  5.1 0.7 add_convert_fusion.1.pick_ref
  5.7 0.1 broadcast_compare_fusion.1
  5.9 0.1 fusion.5
  6.0 0.1 fusion.6
  6.1 0.1 fusion.4
  6.2 0.1 fusion.2
  6.4 0.1 iota_compare_fusion.5
  6.5 0.1 add_bitcast_fusion
  6.6 1.2 add_convert_fusion.mask_ref
  7.8 1.2 fusion.1
  9.1 0.9 pad_maximum_fusion.cos_ref
  9.9 0.9 pad_maximum_fusion.1.sin_ref
  10.8 195.0 %shard_map.118 = bf16[32,8192]{1,0:T(8,128)(2,1)} custom-call(bf16[128,1536]{1,0:T(8,128)(2,1)} %feats_ref.1, bf16[1536,8192]{1,0:T(8,128)(2,1)} %uniting_ref.1, bf16[640,512]{1,0:T(8,128)(2,1)} %fusion.eg_ref, f32[8,128]{1,0:T(8,128)} %concatenate.35.sqe_ref, bf16[16,512]{1,0:T(8,128)(2,1)} %broadcast_in_dim.85.gh_ref, bf16[512,5120]{1,0:T(8,128)(2,1)} %we_hbm.1, ...), custom_call_target="tpu_custom_call" | custom-call | tf_op jit(solution)/shard_map/pallas_call | solution.py:751
  205.8 1.9 copy.25
  (29 shorter events, 0.2 us)
Async XLA Ops:
  0.0 1.2 copy-start.5
  1.2 1.1 copy-start
  1.2 1.1 copy-start.1
  1.3 1.9 copy-start.6
  1.3 2.5 %copy-start.4 = (s32[3,128]{1,0:T(4,128)S(1)}, s32[3,128]{1,0:T(4,128)}, u32[]{:S(2)}) copy-start(s32[3,128]{1,0:T(4,128)} %param.23) | copy-start | bytes 4612
  1.3 2.7 %copy-start.3 = (s32[128]{0:T(128)S(1)}, s32[128]{0:T(128)}, u32[]{:S(2)}) copy-start(s32[128]{0:T(128)} %param.22) | copy-start | bytes 1540
  1.3 3.2 %copy-start.2 = (s32[16]{0:T(128)S(1)}, s32[16]{0:T(128)}, u32[]{:S(2)}) copy-start(s32[16]{0:T(128)} %param.21) | copy-start | bytes 196

commit v4 on v3

--- a/solution.py
+++ b/solution.py
@@ -569,19 +569,20 @@
         kv_get(t, base)
         if first:
             kv_get(steps, 0)
-        keys = kv_ref[:, 0:HD]
-        vals = kv_ref[:, HD : 2 * HD]
+        span = 2 * rows if first else kv_ref.shape[0]
+        keys = kv_ref[0:span, 0:HD]
+        vals = kv_ref[0:span, HD : 2 * HD]
         heads = len(queries)
-        allowed = jnp.concatenate([mask_ref[t]] * heads, axis=0) > 0
+        allowed = jnp.concatenate([mask_ref[t, :, 0:span]] * heads, axis=0) > 0
         scores = lax.dot_general(
             jnp.concatenate(queries, axis=0),
             keys,
             (((1,), (1,)), ((), ())),
             preferred_element_type=f32,
-        ) / math.sqrt(HD)
+        ) * (1.0 / math.sqrt(HD))
         scores = jnp.where(allowed, scores, MASKED)
         expo = jnp.exp(scores - jnp.max(scores, axis=1, keepdims=True))
-        weights = (expo / jnp.sum(expo, axis=1, keepdims=True)).astype(bf16)
+        weights = (expo * (1.0 / jnp.sum(expo, axis=1, keepdims=True))).astype(bf16)
         mixed = jnp.dot(weights, vals, preferred_element_type=f32).astype(bf16)
         for j in range(heads):
             att_ref[t, me, :, j * HD : (j + 1) * HD] = mixed[j * rows : (j + 1) * rows]

time: 208 us -> 208 us (level)
  no operation moved by 1% of the time
where the time goes in v4:
time: 208 us
  Pallas kernels  195 us (94%)
  other arithmetic  9.2 us (4%)
  local copies, waits for them, and re-layouts  3.25 us (2%)
    pallas_call x1, Pallas kernels, local_kernel(): pl.pallas_call(functools.partial(draft_kernel, steps), out_shape=jax.Shap...  195 us

profile of v4, /device:TPU:31, one launch (start us, length us, event | category | flops | bytes accessed | tf_op | source)
XLA Modules:
  0.0 207.5 jit_solution(1053087666801392310)
XLA Ops:
  0.0 1.2 maximum_convert_fusion
  1.2 0.0 copy-start
  1.3 0.0 copy-start.6
  1.3 0.0 copy-start.2
  1.3 1.0 fusion.eg_ref
  2.3 0.2 multiply_reduce_fusion
  2.5 0.6 concatenate.35.sqe_ref
  3.1 0.6 broadcast_in_dim.85.gh_ref
  3.7 0.1 iota_compare_fusion.7
  3.8 0.1 iota_compare_fusion.9
  3.9 0.2 select_reduce_fusion.5
  4.1 0.2 select_reduce_fusion.3
  4.3 0.2 select_reduce_fusion
  4.5 0.1 copy.15
  4.7 0.1 reduce
  4.8 0.1 convert_reduce_fusion
  4.9 0.1 select_reduce_fusion.7
  5.0 0.1 iota_compare_fusion.10
  5.1 0.7 add_convert_fusion.1.pick_ref
  5.7 0.1 broadcast_compare_fusion.1
  5.9 0.1 fusion.5
  6.0 0.1 fusion.6
  6.1 0.1 fusion.4
  6.2 0.1 fusion.2
  6.4 0.1 iota_compare_fusion.5
  6.5 0.1 add_bitcast_fusion
  6.6 1.2 add_convert_fusion.mask_ref
  7.8 1.2 fusion.1
  9.1 0.9 pad_maximum_fusion.cos_ref
  9.9 0.9 pad_maximum_fusion.1.sin_ref
  10.8 194.8 %shard_map.118 = bf16[32,8192]{1,0:T(8,128)(2,1)} custom-call(bf16[128,1536]{1,0:T(8,128)(2,1)} %feats_ref.1, bf16[1536,8192]{1,0:T(8,128)(2,1)} %uniting_ref.1, bf16[640,512]{1,0:T(8,128)(2,1)} %fusion.eg_ref, f32[8,128]{1,0:T(8,128)} %concatenate.35.sqe_ref, bf16[16,512]{1,0:T(8,128)(2,1)} %broadcast_in_dim.85.gh_ref, bf16[512,5120]{1,0:T(8,128)(2,1)} %we_hbm.1, ...), custom_call_target="tpu_custom_call" | custom-call | tf_op jit(solution)/shard_map/pallas_call | solution.py:752
  205.7 1.9 copy.25
  (29 shorter events, 0.2 us)
Async XLA Ops:
  0.0 1.2 copy-start.5
  1.2 1.1 copy-start
  1.2 1.1 copy-start.1
  1.3 1.9 copy-start.6
  1.3 2.5 %copy-start.4 = (s32[3,128]{1,0:T(4,128)S(1)}, s32[3,128]{1,0:T(4,128)}, u32[]{:S(2)}) copy-start(s32[3,128]{1,0:T(4,128)} %param.23) | copy-start | bytes 4612
  1.3 2.7 %copy-start.3 = (s32[128]{0:T(128)S(1)}, s32[128]{0:T(128)}, u32[]{:S(2)}) copy-start(s32[128]{0:T(128)} %param.22) | copy-start | bytes 1540
  1.3 3.2 %copy-start.2 = (s32[16]{0:T(128)S(1)}, s32[16]{0:T(128)}, u32[]{:S(2)}) copy-start(s32[16]{0:T(128)} %param.21) | copy-start | bytes 196
